TPU v7x, 256 devices: a whole 4x4x8 slice. The times are simulated.
256 devices in a mesh: vid: 16 (over y_hi, z), seq: 16 (over x, y_lo, core).
Axes of the slice: x: 4, y: 4 (y_hi: 2, y_lo: 2; y = y_hi * 2 + y_lo), z: 8, core: 2. Of those that a mesh axis runs over, the one named last changes fastest.
Arguments:
- video: bfloat16 [16, 512, 4096], P('vid', 'seq'), may hold values from -8 to 8
- video_length: int32 [16], P('vid'), may hold values from 128 to 512
- prompt: bfloat16 [16, 128, 4096], P('vid', 'seq'), may hold values from -6 to 6
- prompt_length: int32 [16], replicated, may hold values from 32 to 128
- prompt_choice: int32 [16], P('vid'), may hold values from 0 to 15
- ffn_gain: float32 [4096], replicated, may hold values from 0.1 to 1.9
- ffn_gate: bfloat16 [4096, 6144], P(None, 'seq'), may hold values from -0.09375 to 0.09375
- ffn_up: bfloat16 [4096, 6144], P(None, 'seq'), may hold values from -0.09375 to 0.09375
- ffn_down: bfloat16 [6144, 4096], P('seq'), may hold values from -0.078125 to 0.078125
- final_gain: float32 [4096], replicated, may hold values from 0.1 to 1.9
- video_gain: float32 [4096], replicated, may hold values from 0.1 to 1.9
- w_query: bfloat16 [4096, 4096], P('vid', 'seq'), may hold values from -1 to 1
- w_key: bfloat16 [4096, 4096], P('vid', 'seq'), may hold values from -3 to 3
- w_value: bfloat16 [4096, 4096], P('vid', 'seq'), may hold values from -0.09375 to 0.09375
- w_text_key: bfloat16 [4096, 4096], P('vid', 'seq'), may hold values from -0.09375 to 0.09375
- w_text_value: bfloat16 [4096, 4096], P('vid', 'seq'), may hold values from -0.09375 to 0.09375
- w_out: bfloat16 [4096, 4096], P('seq', 'vid'), may hold values from -0.09375 to 0.09375
Outputs:
- updated: bfloat16 [16, 512, 4096], P('vid', 'seq')
Inputs may be any that keep to these rules, and one draw needn't show every extreme that they name: `prompt_choice`: A prompt may serve several videos or none.
All inputs are finite; a program needn't handle non-finite values.
Results may differ from a plain program's by a relative error of at most 0.0085.
Values may be sent and summed in bfloat16 or wider, within the bound.
A program may use at most 128 MiB of HBM per device.

v0:
```python
import jax
import jax.numpy as jnp
from jax import lax
from jax.sharding import PartitionSpec as P

HD = 128
epsilon = 1e-06


def sent_to_all(x, axis):
    devices = lax.axis_size(axis)
    return lax.all_to_all(jnp.broadcast_to(x[None], (devices, *x.shape)), axis, 0, 0, tiled=True)


def laid_out(tiles, dim):
    lengths = list(tiles.shape[1:])
    lengths[dim] *= tiles.shape[0]
    return jnp.moveaxis(tiles, 0, dim).reshape(lengths)


def gathered_copies(x, axis, dim):
    tiles = sent_to_all(x, axis)
    return laid_out(tiles, dim)


def in_blocks(x, dim, devices):
    lengths = x.shape
    tiles = x.reshape(*lengths[:dim], devices, lengths[dim] // devices, *lengths[dim + 1 :])
    return jnp.moveaxis(tiles, dim, 0)


def sent_and_summed(x, axis, dim):
    tiles = in_blocks(x, dim, lax.axis_size(axis))
    arrived = lax.all_to_all(tiles, axis, split_axis=0, concat_axis=0, tiled=True)
    return arrived.astype(jnp.float32).sum(axis=0)


def side_by_side(arrays, axis, dim, along):
    both = jnp.concatenate(arrays, axis=along)
    whole, at, finished = (lax.all_gather(both, axis, axis=dim, tiled=True), 0, [])
    for a in arrays:
        finished.append(lax.slice_in_dim(whole, at, at + a.shape[along], axis=along))
        at += a.shape[along]
    return tuple(finished)


def rms_norm(values, gain):
    return values * lax.rsqrt(jnp.mean(values * values, axis=-1, keepdims=True) + epsilon) * gain


def prompt_path(
    prompt,
    prompt_length,
    prompt_choice,
    ffn_gain,
    ffn_gate,
    ffn_up,
    ffn_down,
    final_gain,
    w_text_key,
    w_text_value,
):
    gathered = gathered_copies(prompt, "seq", 1)[0]
    residual = gathered.astype(jnp.float32)
    ffn_normed = rms_norm(residual, ffn_gain).astype(jnp.bfloat16)
    gate_proj = jnp.dot(ffn_normed, ffn_gate, preferred_element_type=jnp.float32)
    up_proj = jnp.dot(ffn_normed, ffn_up, preferred_element_type=jnp.float32)
    ffn_hidden = (jax.nn.gelu(gate_proj, approximate=True) * up_proj).astype(jnp.bfloat16)
    partial_value = jnp.dot(ffn_hidden, ffn_down, preferred_element_type=jnp.float32)
    share = sent_and_summed(partial_value.astype(jnp.bfloat16), "seq", 0)
    own_rows = prompt[0].astype(jnp.float32)
    text_share = rms_norm(own_rows + share, final_gain).astype(jnp.bfloat16)
    text = gathered_copies(text_share, "seq", 0)
    blocks = side_by_side((w_text_key, w_text_value), "vid", 0, 1)
    key_sum = jnp.dot(text, blocks[0], preferred_element_type=jnp.float32)
    value_sum = jnp.dot(text, blocks[1], preferred_element_type=jnp.float32)
    text_key = key_sum.astype(jnp.bfloat16)[None]
    text_value = value_sum.astype(jnp.bfloat16)[None]
    wanted = prompt_choice[0]
    blocks = side_by_side((text_key, text_value), "vid", 0, 1)
    number = blocks[0].shape[0]
    chosen = jnp.arange(number, dtype=jnp.int32) == wanted
    picked_key = jnp.sum(
        jnp.where(chosen[:, None, None], blocks[0], jnp.zeros_like(blocks[0])), axis=0
    )
    picked_value = jnp.sum(
        jnp.where(chosen[:, None, None], blocks[1], jnp.zeros_like(blocks[1])), axis=0
    )
    prompt_ids = jnp.arange(prompt_length.shape[0], dtype=jnp.int32)
    text_live = jnp.sum(jnp.where(prompt_ids == wanted, prompt_length, 0))
    return (picked_key, picked_value, text_live)


def video_path(residual, video_gain, w_query, w_key, w_value):
    normed = rms_norm(residual, video_gain).astype(jnp.bfloat16)
    whole_rows = lax.all_gather(normed, "seq", axis=0, tiled=True)
    blocks = side_by_side((w_query, w_key, w_value), "vid", 0, 1)
    query_sum, key_sum, value_sum = tuple(
        (
            jnp.dot(whole_rows, blocks[index], preferred_element_type=jnp.float32)
            for index in range(3)
        )
    )
    return (
        query_sum.astype(jnp.bfloat16),
        key_sum.astype(jnp.bfloat16),
        value_sum.astype(jnp.bfloat16),
    )


def local(
    video,
    video_length,
    prompt,
    prompt_length,
    prompt_choice,
    ffn_gain,
    ffn_gate,
    ffn_up,
    ffn_down,
    final_gain,
    video_gain,
    w_query,
    w_key,
    w_value,
    w_text_key,
    w_text_value,
    w_out,
):
    residual = video[0].astype(jnp.float32)
    text_key, text_value, text_live = prompt_path(
        prompt,
        prompt_length,
        prompt_choice,
        ffn_gain,
        ffn_gate,
        ffn_up,
        ffn_down,
        final_gain,
        w_text_key,
        w_text_value,
    )
    query, key_rows, value_rows = video_path(residual, video_gain, w_query, w_key, w_value)
    out_full = gathered_copies(w_out, "vid", 1)
    total_rows = query.shape[0]
    text_rows = text_key.shape[0]
    width_here = query.shape[1]
    head_count = width_here // HD
    frame_length = video_length[0]
    joint_keys = jnp.concatenate([key_rows, text_key], axis=0).reshape(
        total_rows + text_rows, head_count, HD
    )
    joint_values = jnp.concatenate([value_rows, text_value], axis=0).reshape(
        total_rows + text_rows, head_count, HD
    )
    query_heads = query.reshape(total_rows, head_count, HD)
    scores = jnp.einsum(
        "qhd,khd->hqk", query_heads, joint_keys, preferred_element_type=jnp.float32
    ) * HD ** (-0.5)
    position = jnp.arange(total_rows + text_rows, dtype=jnp.int32)
    live_keys = jnp.where(
        position < total_rows, position < frame_length, position - total_rows < text_live
    )
    scores = jnp.where(live_keys[None, None, :], scores, -1e30)
    probs = jax.nn.softmax(scores, axis=-1).astype(jnp.bfloat16)
    attended = jnp.einsum("hqk,khd->qhd", probs, joint_values, preferred_element_type=jnp.float32)
    attended = attended.astype(jnp.bfloat16).reshape(total_rows, width_here)
    local_rows = video.shape[1]
    projected = lax.psum_scatter(
        jnp.dot(attended, out_full, preferred_element_type=jnp.float32).astype(jnp.bfloat16),
        "seq",
        scatter_dimension=0,
        tiled=True,
    ).astype(jnp.float32)
    row_position = lax.axis_index("seq") * local_rows + jnp.arange(local_rows, dtype=jnp.int32)
    row_live = row_position < frame_length
    updated = residual + jnp.where(row_live[:, None], projected, 0.0)
    return updated.astype(jnp.bfloat16)[None]


def solution(mesh):
    in_specs = (
        P("vid", "seq", None),
        P("vid"),
        P("vid", "seq", None),
        P(),
        P("vid"),
        P(),
        P(None, "seq"),
        P(None, "seq"),
        P("seq", None),
        P(),
        P(),
        P("vid", "seq"),
        P("vid", "seq"),
        P("vid", "seq"),
        P("vid", "seq"),
        P("vid", "seq"),
        P("seq", "vid"),
    )
    out_specs = P("vid", "seq", None)
    return jax.shard_map(local, mesh=mesh, in_specs=in_specs, out_specs=out_specs, check_vma=False)
```

profile of v0, /device:TPU:32, one launch (start us, length us, event | category | flops | bytes accessed | tf_op | source)
XLA Modules:
  0.0 484.5 jit_solution(16630161298644301142)
XLA Ops:
  6.5 0.0 copy-start
  6.5 0.0 all-gather.9.cloned.1.call-start
  6.5 1.8 pad_maximum_fusion.2
  8.4 0.0 all-gather.9.cloned.1.call-update
  8.4 0.0 all-gather.11.cloned.1.call-start
  8.5 0.9 broadcast_in_dim.85
  9.4 21.7 %all_to_all.20 = bf16[16,1,8,4096]{3,2,1,0:T(8,128)(2,1)S(1)} all-to-all(bf16[16,1,8,4096]{3,2,1,0:T(8,128)(2,1)S(1)} %broadcast_in_dim.85), channel_id=1, replica_groups=mesh['vid'=16,'seq'=16] {'seq'}, dimensions={0} | all-to-all | bytes 2097152 | tf_op jit(solution)/shard_map/all_to_all | solution.py:12
  31.1 1.0 copy-done.1
  32.1 0.3 fusion.5
  32.4 0.1 rsqrt.29
  32.5 0.0 copy-done.6
  32.5 3.0 fusion.70
  35.5 0.0 copy-done
  35.5 4.7 fusion.1
  40.2 20.2 %all_to_all.21 = bf16[16,8,4096]{2,1,0:T(8,128)(2,1)S(1)} all-to-all(bf16[16,8,4096]{2,1,0:T(8,128)(2,1)} %fusion.1), channel_id=1, replica_groups=mesh['vid'=16,'seq'=16] {'seq'}, dimensions={0} | all-to-all | bytes 2097152 | tf_op jit(solution)/shard_map/all_to_all | solution.py:34
  60.4 0.1 convert_reduce_fusion
  60.6 0.0 copy-done.4
  60.6 0.1 multiply_reduce_fusion
  60.7 0.0 copy-done.7
  60.7 0.1 fusion.76
  60.8 0.1 broadcast_in_dim.87
  60.9 20.3 %all_to_all.22 = bf16[16,8,4096]{2,1,0:T(8,128)(2,1)} all-to-all(bf16[16,8,4096]{2,1,0:T(8,128)(2,1)S(1)} %broadcast_in_dim.87), channel_id=1, replica_groups=mesh['vid'=16,'seq'=16] {'seq'}, dimensions={0} | all-to-all | bytes 2097152 | tf_op jit(solution)/shard_map/all_to_all | solution.py:12
  81.2 44.5 %all-gather.9.cloned.1.call-done = bf16[4096,512]{1,0:T(8,128)(2,1)} async-done(((bf16[256,512]{1,0:T(8,128)(2,1)}), bf16[4096,512]{1,0:T(8,128)(2,1)}) %all-gather.9.cloned.1.call-update) | async-done | bytes 4194320 | tf_op jit(solution)/shard_map/all_gather | solution.py:40
  125.7 2.4 fusion.38
  128.2 0.0 copy-done.3
  128.2 0.0 copy-start.2
  128.2 0.0 copy-start.8
  128.2 0.0 copy-start.5
  128.2 2.1 fusion.41
  130.3 0.7 pad_maximum_fusion.3
  131.0 0.0 all-gather.11.cloned.1.call-update
  131.0 0.0 all-gather.5.cloned.1.call-start
  131.0 0.0 copy-done.2
  131.0 0.2 fusion.48
  131.2 0.0 copy-done.8
  131.2 0.8 fusion.50
  132.1 0.0 all-gather.5.cloned.1.call-update
  132.1 0.0 all-gather.7.cloned.1.call-start
  132.1 0.0 copy-done.5
  132.1 1.7 pad_maximum_fusion
  133.9 0.0 all-gather.7.cloned.1.call-update
  133.9 1.0 copy.32
  134.9 1.6 broadcast_in_dim.93
  136.5 5.0 %all-to-all-start.3 = ((bf16[16,256,256]{1,2,0:T(8,128)(2,1)}), bf16[16,256,256]{1,2,0:T(8,128)(2,1)}, u32[]{:S(2)}, u32[]{:S(2)}) async-start(bf16[16,256,256]{1,2,0:T(8,128)(2,1)} %broadcast_in_dim.93), calls=%async_computation.3 | async-start | bytes 4194304 | tf_op jit(solution)/shard_map/all_to_all | solution.py:12
  141.5 0.2 reduce-scatter.2.cloned.1.call-start
  143.0 0.0 copy-done.10
  143.1 0.7 select_reduce_fusion
  143.8 0.7 fusion.81
  144.5 81.8 %all-gather.11.cloned.1.call-done = bf16[16,256,256]{2,1,0:T(8,128)(2,1)} async-done(((bf16[1,256,256]{2,1,0:T(8,128)(2,1)}), bf16[16,256,256]{2,1,0:T(8,128)(2,1)}) %all-gather.11.cloned.1.call-update) | async-done | bytes 2097168 | tf_op jit(solution)/shard_map/all_gather | solution.py:40
  226.3 1.9 fusion.44
  228.2 37.0 %all-gather.5.cloned.1.call-done = bf16[512,4096]{1,0:T(8,128)(2,1)} async-done(((bf16[32,4096]{1,0:T(8,128)(2,1)}), bf16[512,4096]{1,0:T(8,128)(2,1)}) %all-gather.5.cloned.1.call-update) | async-done | bytes 4194320 | tf_op jit(solution)/shard_map/all_gather | solution.py:96
  265.2 118.0 %all-gather.7.cloned.1.call-done = bf16[4096,768]{1,0:T(8,128)(2,1)} async-done(((bf16[256,768]{1,0:T(8,128)(2,1)}), bf16[4096,768]{1,0:T(8,128)(2,1)}) %all-gather.7.cloned.1.call-update) | async-done | bytes 6291472 | tf_op jit(solution)/shard_map/all_gather | solution.py:40
  383.2 4.1 fusion.22
  387.4 0.7 pad_maximum_fusion.1
  388.1 1.9 copy.34
  390.0 5.0 %fusion.25 = bf16[512,256]{0,1:T(8,128)(2,1)} fusion(bf16[512,4096]{1,0:T(8,128)(2,1)} %all-gather.5.cloned.1.call-done, bf16[4096,768]{1,0:T(8,128)(2,1)} %all-gather.7.cloned.1.call-done), kind=kOutput, calls=%fused_computation.31 | convolution fusion | flops 1073872896 | bytes 6553600 | tf_op jit(solution)/shard_map/dot_general | solution.py:100
  395.0 3.6 fusion.28
  398.6 2.2 fusion.91
  400.7 3.2 fusion.21
  403.9 0.0 all-to-all-done.3
  403.9 4.9 %convolution_convert_fusion = bf16[512,4096]{1,0:T(8,128)(2,1)} fusion(bf16[512,256]{0,1:T(8,128)(2,1)} %bitcast.94, bf16[256,4096]{0,1:T(8,128)(2,1)} %bitcast.17), kind=kOutput, calls=%fused_computation.1 | convolution fusion | flops 1075838976 | bytes 6553600 | tf_op jit(solution)/shard_map/dot_general | solution.py:170
  408.8 0.0 reduce-scatter.2.cloned.1.call-update
  408.9 67.3 %reduce-scatter.2.cloned.1.call-done = bf16[32,4096]{1,0:T(8,128)(2,1)} async-done(((bf16[512,4096]{1,0:T(8,128)(2,1)}), bf16[32,4096]{1,0:T(8,128)(2,1)}) %reduce-scatter.2.cloned.1.call-update) | async-done | bytes 262160 | tf_op jit(solution)/shard_map/reduce_scatter | solution.py:169
  476.2 1.8 fusion.59
  (13 shorter events, 0.1 us)
Async XLA Ops:
  6.5 29.0 %copy-start = (bf16[384,4096]{1,0:T(8,128)(2,1)S(1)}, bf16[384,4096]{1,0:T(8,128)(2,1)}, u32[]{:S(2)}) copy-start(bf16[384,4096]{1,0:T(8,128)(2,1)} %param.25) | copy-start | bytes 9437188
  6.5 25.9 %copy-start.6 = (f32[4096]{0:T(1024)S(1)}, f32[4096]{0:T(1024)}, u32[]{:S(2)}) copy-start(f32[4096]{0:T(1024)} %param.22) | copy-start | bytes 49156
  6.5 119.2 %all-gather.9.cloned.1.call-start = ((), (), s32[]{:S(2)}) async-start(), calls=%async_computation.7 | async-start | bytes 4456448 | tf_op jit(solution)/shard_map/all_gather | solution.py:40
  8.4 217.9 %all-gather.11.cloned.1.call-start = ((), (), s32[]{:S(2)}) async-start(), calls=%async_computation.8 | async-start | bytes 2228224 | tf_op jit(solution)/shard_map/all_gather | solution.py:40
  31.1 1.0 copy-start.1
  40.2 20.4 %copy-start.4 = (bf16[1,8,4096]{2,1,0:T(8,128)(2,1)S(1)}, bf16[1,8,4096]{2,1,0:T(8,128)(2,1)}, u32[]{:S(2)}) copy-start(bf16[1,8,4096]{2,1,0:T(8,128)(2,1)} %param.19) | copy-start | bytes 196612
  40.2 20.5 %copy-start.7 = (f32[4096]{0:T(1024)S(1)}, f32[4096]{0:T(1024)}, u32[]{:S(2)}) copy-start(f32[4096]{0:T(1024)} %param.26) | copy-start | bytes 49156
  125.7 2.4 copy-start.3
  128.2 2.9 copy-start.2
  128.2 3.0 copy-start.8
  128.2 3.9 copy-start.5
  131.0 134.2 %all-gather.5.cloned.1.call-start = ((), (), s32[]{:S(2)}) async-start(), calls=%async_computation.5 | async-start | bytes 4456448 | tf_op jit(solution)/shard_map/all_gather | solution.py:96
  132.1 251.2 %all-gather.7.cloned.1.call-start = ((), (), s32[]{:S(2)}) async-start(), calls=%async_computation.6 | async-start | bytes 6684672 | tf_op jit(solution)/shard_map/all_gather | solution.py:40
  136.5 6.6 %copy-start.10 = (s32[16]{0:T(128)S(1)}, s32[16]{0:T(128)}, u32[]{:S(2)}) copy-start(s32[16]{0:T(128)} %param.20) | copy-start | bytes 196
  136.5 267.4 %all-to-all-start.3 = ((bf16[16,256,256]{1,2,0:T(8,128)(2,1)}), bf16[16,256,256]{1,2,0:T(8,128)(2,1)}, u32[]{:S(2)}, u32[]{:S(2)}) async-start(bf16[16,256,256]{1,2,0:T(8,128)(2,1)} %broadcast_in_dim.93), calls=%async_computation.3 | async-start | bytes 4194304 | tf_op jit(solution)/shard_map/all_to_all | solution.py:12
  141.5 334.7 %reduce-scatter.2.cloned.1.call-start = ((), (), s32[]{:S(2)}) async-start(), calls=%async_computation.9 | async-start | bytes 4456448 | tf_op jit(solution)/shard_map/reduce_scatter | solution.py:169
  390.0 5.0 %copy-start.9 = (bf16[512,4096]{1,0:T(8,128)(2,1)S(1)}, bf16[512,4096]{1,0:T(8,128)(2,1)}, u32[]{:S(2)}) copy-start(bf16[512,4096]{1,0:T(8,128)(2,1)} %all-gather.5.cloned.1.call-done) | copy-start | bytes 12582916
Sparse Core Ops, SparseCore 0:
  9.9 115.7 all-gather.8
  131.1 95.1 all-gather.10
  228.1 37.0 all-gather.4
  267.7 115.5 all-gather.6
  409.0 67.1 reduce-scatter.1
where the time goes:
time: 485 us
  waiting for transfers between devices  349 us (72%)
  blocking collectives  62.2 us (13%)
  matrix products  35.2 us (7%)
  between operations  14.6 us (3%)
  other arithmetic  11.8 us (2%)
  local copies, waits for them, and re-layouts  6.59 us (1%)
  starting transfers between devices  5.37 us (1%)
    all_gather x3, waiting for transfers between devices, side_by_side(): lax.all_gather(both, axis, axis=dim, tiled=True)  244 us
    reduce_scatter x1, waiting for transfers between devices, local(): lax.psum_scatter(jnp.dot(attended, out_full, preferred_element_type=jnp.f...  67.3 us
    all_to_all x2, blocking collectives, sent_to_all(): lax.all_to_all(jnp.broadcast_to(x[None], (devices, *x.shape)), axis, 0, 0...  42 us
    all_gather x1, waiting for transfers between devices, video_path(): whole_rows = lax.all_gather(normed, 'seq', axis=0, tiled=True)  37 us
    all_to_all x1, blocking collectives, sent_and_summed(): lax.all_to_all(tiles, axis, split_axis=0, concat_axis=0, tiled=True)  20.2 us
    dot_general x3, matrix products, video_path(): jnp.dot(whole_rows, blocks[index], preferred_element_type=jnp.float32)  12.7 us
  transfers between devices with their start and end apart: 6, of which 5 were waited for; matrix products, arithmetic and copies ran while one was open for 8% of the time, Pallas kernels for 0%

commit v1 on v0

--- a/solution.py
+++ b/solution.py
@@ -93,7 +93,9 @@
 
 def video_path(residual, video_gain, w_query, w_key, w_value):
     normed = rms_norm(residual, video_gain).astype(jnp.bfloat16)
-    whole_rows = lax.all_gather(normed, "seq", axis=0, tiled=True)
+    whole_rows = jnp.concatenate(
+        lax.all_to_all(jnp.stack([normed] * lax.axis_size("seq")), "seq", 0, 0), axis=0
+    )
     blocks = side_by_side((w_query, w_key, w_value), "vid", 0, 1)
     query_sum, key_sum, value_sum = tuple(
         (

time: 485 us -> 479 us (0.988)
  waiting for transfers between devices: 349 us -> 334 us
  starting transfers between devices: 5.37 us -> 11.4 us
    all_to_all x0 -> x1, waiting for transfers between devices: none -> 51.2 us  [video_path(): lax.all_to_all(jnp.stack([normed] * lax.axis_size('seq')), 'seq', 0, 0)]
    all_gather x1 -> x0, waiting for transfers between devices: 37 us -> none  [video_path(): whole_rows = lax.all_gather(normed, 'seq', axis=0, tiled=True)]
    all_gather x3, waiting for transfers between devices: 244 us -> 215 us  [side_by_side(): lax.all_gather(both, axis, axis=dim, tiled=True)]
  transfers between devices with their start and end apart: 6 -> 6, of which waited for: 5 -> 5; matrix products, arithmetic and copies ran while one was open for 8% -> 9% of each run, Pallas kernels for 0% -> 0%
where the time goes in v1:
time: 479 us
  waiting for transfers between devices  334 us (70%)
  blocking collectives  62.2 us (13%)
  matrix products  36.3 us (8%)
  between operations  14.6 us (3%)
  starting transfers between devices  11.4 us (2%)
  other arithmetic  10.9 us (2%)
  local copies, waits for them, and re-layouts  9.18 us (2%)
    all_gather x3, waiting for transfers between devices, side_by_side(): lax.all_gather(both, axis, axis=dim, tiled=True)  215 us
    reduce_scatter x1, waiting for transfers between devices, local(): lax.psum_scatter(jnp.dot(attended, out_full, preferred_element_type=jnp.f...  67.4 us
    all_to_all x1, waiting for transfers between devices, video_path(): lax.all_to_all(jnp.stack([normed] * lax.axis_size('seq')), 'seq', 0, 0)  51.2 us
    all_to_all x2, blocking collectives, sent_to_all(): lax.all_to_all(jnp.broadcast_to(x[None], (devices, *x.shape)), axis, 0, 0...  42 us
    all_to_all x1, blocking collectives, sent_and_summed(): lax.all_to_all(tiles, axis, split_axis=0, concat_axis=0, tiled=True)  20.2 us
    dot_general x3, matrix products, video_path(): jnp.dot(whole_rows, blocks[index], preferred_element_type=jnp.float32)  13.8 us
  transfers between devices with their start and end apart: 6, of which 5 were waited for; matrix products, arithmetic and copies ran while one was open for 9% of the time, Pallas kernels for 0%

profile of v1, /device:TPU:32, one launch (start us, length us, event | category | flops | bytes accessed | tf_op | source)
XLA Modules:
  0.0 478.5 jit_solution(7748374212029672043)
XLA Ops:
  6.5 0.0 copy-start
  6.5 0.0 all-gather.6.cloned.1.call-start
  6.5 1.8 pad_maximum_fusion.2
  8.4 0.0 all-gather.6.cloned.1.call-update
  8.4 0.0 all-gather.8.cloned.1.call-start
  8.5 0.9 broadcast_in_dim.85
  9.4 21.7 %all_to_all.25 = bf16[16,1,8,4096]{3,2,1,0:T(8,128)(2,1)S(1)} all-to-all(bf16[16,1,8,4096]{3,2,1,0:T(8,128)(2,1)S(1)} %broadcast_in_dim.85), channel_id=1, replica_groups=mesh['vid'=16,'seq'=16] {'seq'}, dimensions={0} | all-to-all | bytes 2097152 | tf_op jit(solution)/shard_map/all_to_all | solution.py:12
  31.1 1.0 copy-done.1
  32.1 0.3 fusion.5
  32.4 0.1 rsqrt.29
  32.5 0.0 copy-done.6
  32.5 3.0 fusion.73
  35.5 0.0 copy-done
  35.5 4.7 fusion.1
  40.2 20.2 %all_to_all.26 = bf16[16,8,4096]{2,1,0:T(8,128)(2,1)S(1)} all-to-all(bf16[16,8,4096]{2,1,0:T(8,128)(2,1)} %fusion.1), channel_id=1, replica_groups=mesh['vid'=16,'seq'=16] {'seq'}, dimensions={0} | all-to-all | bytes 2097152 | tf_op jit(solution)/shard_map/all_to_all | solution.py:34
  60.4 0.1 convert_reduce_fusion
  60.6 0.0 copy-done.4
  60.6 0.1 multiply_reduce_fusion
  60.7 0.0 copy-done.7
  60.7 0.1 fusion.79
  60.8 0.1 broadcast_in_dim.87
  60.9 20.3 %all_to_all.27 = bf16[16,8,4096]{2,1,0:T(8,128)(2,1)} all-to-all(bf16[16,8,4096]{2,1,0:T(8,128)(2,1)S(1)} %broadcast_in_dim.87), channel_id=1, replica_groups=mesh['vid'=16,'seq'=16] {'seq'}, dimensions={0} | all-to-all | bytes 2097152 | tf_op jit(solution)/shard_map/all_to_all | solution.py:12
  81.2 44.5 %all-gather.6.cloned.1.call-done = bf16[4096,512]{1,0:T(8,128)(2,1)} async-done(((bf16[256,512]{1,0:T(8,128)(2,1)}), bf16[4096,512]{1,0:T(8,128)(2,1)}) %all-gather.6.cloned.1.call-update) | async-done | bytes 4194320 | tf_op jit(solution)/shard_map/all_gather | solution.py:40
  125.7 2.4 fusion.38
  128.2 0.0 copy-done.3
  128.2 0.0 copy-start.5
  128.2 0.0 copy-start.2
  128.2 0.0 copy-start.8
  128.2 2.1 fusion.41
  130.3 0.7 pad_maximum_fusion.3
  131.0 0.0 all-gather.8.cloned.1.call-update
  131.0 0.0 all-gather.4.cloned.1.call-start
  131.0 0.0 copy-done.5
  131.0 1.7 pad_maximum_fusion
  132.8 0.0 all-gather.4.cloned.1.call-update
  132.8 0.0 copy-done.2
  132.8 0.2 fusion.50
  133.0 0.0 copy-done.8
  133.0 0.1 fusion.61
  133.1 2.6 stack.5
  135.7 4.5 all-to-all-start
  140.3 1.0 copy.32
  141.3 51.2 %all-to-all-done = bf16[16,32,4096]{2,1,0:T(8,128)(2,1)} async-done(((bf16[16,32,4096]{2,1,0:T(8,128)(2,1)}), bf16[16,32,4096]{2,1,0:T(8,128)(2,1)}, u32[]{:S(2)}, u32[]{:S(2)}) %all-to-all-start) | async-done | bytes 4194336 | tf_op jit(solution)/shard_map/all_to_all | solution.py:97
  192.5 1.6 broadcast_in_dim.93
  194.0 6.5 %all-to-all-start.4 = ((bf16[16,256,256]{1,2,0:T(8,128)(2,1)}), bf16[16,256,256]{1,2,0:T(8,128)(2,1)}, u32[]{:S(2)}, u32[]{:S(2)}) async-start(bf16[16,256,256]{1,2,0:T(8,128)(2,1)} %broadcast_in_dim.93), calls=%async_computation.4 | async-start | bytes 4194304 | tf_op jit(solution)/shard_map/all_to_all | solution.py:12
  200.6 0.2 reduce-scatter.2.cloned.1.call-start
  202.1 0.0 copy-done.9
  202.1 0.6 select_reduce_fusion
  202.8 0.6 fusion.84
  203.4 51.4 %all-gather.8.cloned.1.call-done = bf16[16,256,256]{2,1,0:T(8,128)(2,1)} async-done(((bf16[1,256,256]{2,1,0:T(8,128)(2,1)}), bf16[16,256,256]{2,1,0:T(8,128)(2,1)}) %all-gather.8.cloned.1.call-update) | async-done | bytes 2097168 | tf_op jit(solution)/shard_map/all_gather | solution.py:40
  254.8 1.9 fusion.44
  256.7 119.3 %all-gather.4.cloned.1.call-done = bf16[4096,768]{1,0:T(8,128)(2,1)} async-done(((bf16[256,768]{1,0:T(8,128)(2,1)}), bf16[4096,768]{1,0:T(8,128)(2,1)}) %all-gather.4.cloned.1.call-update) | async-done | bytes 6291472 | tf_op jit(solution)/shard_map/all_gather | solution.py:40
  376.1 4.1 fusion.22
  380.2 0.7 pad_maximum_fusion.1
  380.9 1.9 copy.34
  382.8 4.9 %fusion.25 = bf16[512,256]{0,1:T(8,128)(2,1)} fusion(bf16[512,4096]{1,0:T(8,128)(2,1)} %bitcast.3, bf16[4096,768]{1,0:T(8,128)(2,1)} %all-gather.4.cloned.1.call-done), kind=kOutput, calls=%fused_computation.31 | convolution fusion | flops 1073872896 | bytes 6553600 | tf_op jit(solution)/shard_map/dot_general | solution.py:102
  387.7 4.8 %fusion.28 = bf16[512,256]{1,0:T(8,128)(2,1)} fusion(bf16[512,4096]{1,0:T(8,128)(2,1)} %bitcast.3, bf16[4096,768]{1,0:T(8,128)(2,1)} %all-gather.4.cloned.1.call-done), kind=kOutput, calls=%fused_computation.32 | convolution fusion | flops 1073872896 | bytes 6553600 | tf_op jit(solution)/shard_map/dot_general | solution.py:102
  392.5 2.2 fusion.94
  394.6 3.2 fusion.21
  397.8 0.0 all-to-all-done.4
  397.8 4.9 %convolution_convert_fusion = bf16[512,4096]{1,0:T(8,128)(2,1)} fusion(bf16[512,256]{0,1:T(8,128)(2,1)} %bitcast.104, bf16[256,4096]{0,1:T(8,128)(2,1)} %bitcast.18), kind=kOutput, calls=%fused_computation.1 | convolution fusion | flops 1075838976 | bytes 6553600 | tf_op jit(solution)/shard_map/dot_general | solution.py:172
  402.8 0.0 reduce-scatter.2.cloned.1.call-update
  402.8 67.4 %reduce-scatter.2.cloned.1.call-done = bf16[32,4096]{1,0:T(8,128)(2,1)} async-done(((bf16[512,4096]{1,0:T(8,128)(2,1)}), bf16[32,4096]{1,0:T(8,128)(2,1)}) %reduce-scatter.2.cloned.1.call-update) | async-done | bytes 262160 | tf_op jit(solution)/shard_map/reduce_scatter | solution.py:171
  470.2 1.8 fusion.62
  (11 shorter events, 0.0 us)
Async XLA Ops:
  6.5 29.0 %copy-start = (bf16[384,4096]{1,0:T(8,128)(2,1)S(1)}, bf16[384,4096]{1,0:T(8,128)(2,1)}, u32[]{:S(2)}) copy-start(bf16[384,4096]{1,0:T(8,128)(2,1)} %param.25) | copy-start | bytes 9437188
  6.5 25.9 %copy-start.6 = (f32[4096]{0:T(1024)S(1)}, f32[4096]{0:T(1024)}, u32[]{:S(2)}) copy-start(f32[4096]{0:T(1024)} %param.22) | copy-start | bytes 49156
  6.5 119.2 %all-gather.6.cloned.1.call-start = ((), (), s32[]{:S(2)}) async-start(), calls=%async_computation.7 | async-start | bytes 4456448 | tf_op jit(solution)/shard_map/all_gather | solution.py:40
  8.4 246.4 %all-gather.8.cloned.1.call-start = ((), (), s32[]{:S(2)}) async-start(), calls=%async_computation.8 | async-start | bytes 2228224 | tf_op jit(solution)/shard_map/all_gather | solution.py:40
  31.1 1.0 copy-start.1
  40.2 20.4 %copy-start.4 = (bf16[1,8,4096]{2,1,0:T(8,128)(2,1)S(1)}, bf16[1,8,4096]{2,1,0:T(8,128)(2,1)}, u32[]{:S(2)}) copy-start(bf16[1,8,4096]{2,1,0:T(8,128)(2,1)} %param.19) | copy-start | bytes 196612
  40.2 20.5 %copy-start.7 = (f32[4096]{0:T(1024)S(1)}, f32[4096]{0:T(1024)}, u32[]{:S(2)}) copy-start(f32[4096]{0:T(1024)} %param.26) | copy-start | bytes 49156
  125.7 2.4 copy-start.3
  128.2 2.9 copy-start.5
  128.2 4.6 copy-start.2
  128.2 4.8 %copy-start.8 = (f32[4096]{0:T(1024)S(1)}, f32[4096]{0:T(1024)}, u32[]{:S(2)}) copy-start(f32[4096]{0:T(1024)} %param.27) | copy-start | bytes 49156
  131.0 245.1 %all-gather.4.cloned.1.call-start = ((), (), s32[]{:S(2)}) async-start(), calls=%async_computation.6 | async-start | bytes 6684672 | tf_op jit(solution)/shard_map/all_gather | solution.py:40
  135.7 56.7 %all-to-all-start = ((bf16[16,32,4096]{2,1,0:T(8,128)(2,1)}), bf16[16,32,4096]{2,1,0:T(8,128)(2,1)}, u32[]{:S(2)}, u32[]{:S(2)}) async-start(bf16[16,32,4096]{2,1,0:T(8,128)(2,1)} %stack.5), calls=%async_computation | async-start | bytes 8388608 | tf_op jit(solution)/shard_map/all_to_all | solution.py:97
  194.0 8.1 %copy-start.9 = (s32[16]{0:T(128)S(1)}, s32[16]{0:T(128)}, u32[]{:S(2)}) copy-start(s32[16]{0:T(128)} %param.20) | copy-start | bytes 196
  194.0 203.8 %all-to-all-start.4 = ((bf16[16,256,256]{1,2,0:T(8,128)(2,1)}), bf16[16,256,256]{1,2,0:T(8,128)(2,1)}, u32[]{:S(2)}, u32[]{:S(2)}) async-start(bf16[16,256,256]{1,2,0:T(8,128)(2,1)} %broadcast_in_dim.93), calls=%async_computation.4 | async-start | bytes 4194304 | tf_op jit(solution)/shard_map/all_to_all | solution.py:12
  200.6 269.6 %reduce-scatter.2.cloned.1.call-start = ((), (), s32[]{:S(2)}) async-start(), calls=%async_computation.9 | async-start | bytes 4456448 | tf_op jit(solution)/shard_map/reduce_scatter | solution.py:171
Sparse Core Ops, SparseCore 0:
  9.9 115.7 all-gather.5
  131.1 123.6 all-gather.7
  257.4 118.6 all-gather.3
  402.9 67.2 reduce-scatter.1
